TPU v7x, 32 devices: a whole 2x2x4 slice. The times are simulated.
32 devices in a mesh: seq: 8 (over z, x), tp: 4 (over y, core).
Axes of the slice: x: 2, y: 2, z: 4, core: 2. Of those that a mesh axis runs over, the one named last changes fastest.
Arguments:
- tokens: bfloat16 [4096, 2048], P('seq', 'tp'), may hold values from -6 to 6
- norm_gain: float32 [2048], replicated, may hold values from 0.1 to 1.9
- w_query: bfloat16 [2048, 2048], P(None, 'tp'), may hold values from -0.125 to 0.125
- w_keyval: bfloat16 [2048, 256], replicated, may hold values from -0.125 to 0.125
- w_out: bfloat16 [2048, 2048], P('tp'), may hold values from -0.5 to 0.5
- span_lens: int32 [8], P('seq'), may hold values from 1 to 512, 3072 in all
- cached_lens: int32 [8], P('seq'), may hold values from 1 to 1536, 6144 in all
- old_table: int32 [8, 8], P('seq'), may hold values from 0 to 7, each once within a row
- new_table: int32 [8, 8], P('seq'), may hold values from 0 to 7, each once within a row
- old_cache: bfloat16 [64, 256, 256], P('seq', 'tp'), may hold values from -720 to 720
Outputs:
- mixed: bfloat16 [4096, 2048], P('seq', 'tp')
- new_cache: bfloat16 [64, 256, 256], P('seq', 'tp')
Inputs may be any that keep to these rules, and one draw needn't show every extreme that they name: Request r's new tokens are the first span_lens[r] of its 512 rows. `old_table`: each row names every device once: each device holds exactly one block of every request. `new_table`: each row names every device once: each device receives exactly one block of every request.
All inputs are finite; a program needn't handle non-finite values. No bound on the sum of `span_lens` or of `cached_lens` on one device may be relied on, other than what follows from the above.
Results may differ from a plain program's by a relative error of at most 0.012.
The roundings to bfloat16 on the way count: a program that leaves them out, or rounds other values in their place, can miss the bound.
Values may be sent and summed in bfloat16 or wider, within the bound.
No kernel may reach another device: no remote copies, remote signals or barrier semaphores. Data moves between devices by JAX's collectives and lax.ppermute only.
A program may use at most 128 MiB of HBM per device.

v0:
```python
import functools
import math

import jax
import jax.numpy as jnp
from jax import lax
from jax.experimental import pallas as pl
from jax.experimental.pallas import tpu as pltpu
from jax.sharding import PartitionSpec as P

EPSILON = 1e-05
MASKED = -1e30
CHUNKS = 2
PART_ROWS = 256
ROW_TILE = 128
KEY_TILE = 128
NORM_ROWS = 128
MIB = 51
PROJECT_MIB = 50.375
ATTEND_MIB = 49.75
SAFE = 60.0
F32 = jnp.float32
BF16 = jnp.bfloat16

VMEM = pl.BlockSpec(memory_space=pltpu.VMEM)
SMEM = pl.BlockSpec(memory_space=pltpu.SMEM)
HBM = pl.BlockSpec(memory_space=pltpu.HBM)


def dot(a, b):
    return lax.dot_general(a, b, (((1,), (0,)), ((), ())), preferred_element_type=F32)


def dot_t(a, b):
    return lax.dot_general(a, b, (((1,), (1,)), ((), ())), preferred_element_type=F32)


def collect_kernel(*refs):
    for k, pair_ref in enumerate(refs[:-1]):
        refs[-1][k] = pair_ref[1]


def place_kernel(got_ref, *refs):
    me = lax.axis_index("seq")
    for k, pair_ref in enumerate(refs[:-1]):
        refs[-1][me ^ (2 * k)] = pair_ref[0]
        refs[-1][me ^ (2 * k + 1)] = got_ref[k]


def order_kernel(share, plan_ref, arrived_ref, out_ref):
    rows, count = out_ref.shape[0], arrived_ref.shape[0]
    row = lax.broadcasted_iota(jnp.int32, (rows, 128), 0)
    block = row // share
    holder = jnp.zeros_like(block)
    for b in range(rows // share):
        holder = jnp.where(block == b, plan_ref[2 + b], holder)
    index = (holder * share + row % share)[:, :1]
    column = lax.broadcasted_iota(jnp.int32, (rows, count), 1)
    pick = jnp.where(column == index, 1.0, 0.0).astype(BF16)
    out_ref[...] = dot(pick, arrived_ref[...]).astype(BF16)


def extend_kernel(share, block_rows, plan_ref, kv_ref, arrived_ref, *out_refs):
    rows = arrived_ref.shape[0]
    groups = rows // share
    held, span = plan_ref[0], plan_ref[1]
    me = lax.axis_index("seq") if len(out_refs) > 1 else 0
    row = lax.broadcasted_iota(jnp.int32, (rows, 128), 0)
    target = row // share
    block, holder = jnp.zeros_like(row), jnp.zeros_like(row)
    for b in range(groups):
        hit = target == plan_ref[2 + groups + b] ^ me
        block = jnp.where(hit, b, block)
        holder = jnp.where(hit, plan_ref[2 + b], holder)
    position = block * block_rows + lax.axis_index("tp") * share + row % share
    old_row = jnp.where(position < held, holder * share + row % share, -1)[:, :1]
    fresh = position - held
    new_row = jnp.where((fresh >= 0) & (fresh < span), fresh, -1)[:, :1]
    column = lax.broadcasted_iota(jnp.int32, (rows, rows), 1)
    total = dot(jnp.where(column == old_row, 1.0, 0.0).astype(BF16), arrived_ref[...])
    column = lax.broadcasted_iota(jnp.int32, (rows, kv_ref.shape[0]), 1)
    total += dot(jnp.where(column == new_row, 1.0, 0.0).astype(BF16), kv_ref[...])
    total = total.astype(BF16)
    if len(out_refs) == 1:
        out_refs[0][...] = total
        return
    for slot in range(groups):
        out_refs[slot // 2][slot % 2] = total[slot * share : (slot + 1) * share]


def project_kernel(
    x0,
    x1,
    x2,
    x3,
    gain_ref,
    wq_hbm,
    wkv_hbm,
    q_ref,
    kv_ref,
    values_ref,
    limits_ref,
    normed,
    wq_ref,
    wkv_ref,
    sems,
):
    pieces = (x0, x1, x2, x3)
    me = lax.axis_index("tp")
    rows, width = x0.shape
    features = width * len(pieces)
    hd = kv_ref.shape[1] // 2
    heads = wq_ref.shape[1] // hd
    loads = []
    for hbm, to in ((wkv_hbm, wkv_ref), (wq_hbm, wq_ref)):
        for j in range(len(pieces)):
            at = pl.ds(j * width, width)
            loads.append(pltpu.make_async_copy(hbm.at[at], to.at[at], sems.at[len(loads)]))
            loads[-1].start()

    for step in range(0, rows, NORM_ROWS):
        at = pl.ds(step, NORM_ROWS)
        values = [piece[at, :].astype(F32) for piece in pieces]
        average = jnp.sum(sum(values), axis=1, keepdims=True) / features
        centred = [v - average for v in values]
        spread = jnp.sum(sum(v * v for v in centred), axis=1, keepdims=True) / features
        scale = lax.rsqrt(spread + EPSILON)
        for j, v in enumerate(centred):
            owner = me ^ j
            to = pl.ds(pl.multiple_of(owner * width, width), width)
            normed[at, to] = (v * scale * gain_ref[owner]).astype(BF16)
    for load in loads[: len(pieces)]:
        load.wait()
    keyval = dot(normed[...], wkv_ref[...]).astype(BF16)
    kv_ref[...] = keyval
    values_ref[:, hd:] = keyval[:, hd:]
    values_ref[:, :hd] = jnp.ones((rows, hd), BF16)
    limits_ref[0] = longest(keyval[:, :hd])
    for load in loads[len(pieces) :]:
        load.wait()
    query = dot(normed[...], wq_ref[...]).astype(BF16)
    for start in range(0, rows, ROW_TILE):
        for h in range(heads):
            q_ref[pl.ds(start * heads + h * ROW_TILE, ROW_TILE), :] = query[
                start : start + ROW_TILE, h * hd : (h + 1) * hd
            ]
    limits_ref[1] = longest(q_ref[...])


def longest(x):
    squares = dot(x * x, jnp.ones((x.shape[1], 128), BF16))
    return jnp.max(squares.reshape(-1, 8, 128), axis=0)


def attend_kernel(share, block_rows, start_row, rows, plan_ref, q_ref, kv_ref, new_ref, *refs):
    limits_ref, pieces, wout_hbm = refs[0], refs[1:5], refs[5]
    if start_row:
        old_ref, old_limit_ref = refs[6:8]
    else:
        old_ref, old_limit_ref = refs[10:12]
    total, high, context, wout, sem = refs[-5:]
    at = 8 if start_row else 6
    count = (len(refs) - 5 - at) // 2 if start_row else 2
    far_refs, near_refs = refs[at : at + count], refs[at + count : at + 2 * count]
    me = lax.axis_index("tp")
    held, span = plan_ref[0], plan_ref[1]
    piece_rows, width = pieces[0].shape
    hd = width // 2
    heads = q_ref.shape[0] // kv_ref.shape[0]
    load = pltpu.make_async_copy(wout_hbm, wout, sem)
    load.start()

    group = KEY_TILE * len(pieces)
    most = piece_rows // KEY_TILE
    tiles = (held + group - 1) // group
    if not start_row:
        row = lax.broadcasted_iota(jnp.int32, (KEY_TILE, hd), 0)
        place = row // share * block_rows + row % share
        limit = jnp.zeros((8, 128), F32)

        def lay(i, whole):
            source = pl.ds(i * KEY_TILE, KEY_TILE)
            for j, piece in enumerate(pieces):
                at = pl.ds(i * group + j * KEY_TILE, KEY_TILE)
                if whole:
                    old_ref[at, hd:] = piece[source, hd:]
                    old_ref[at, :hd] = jnp.ones((KEY_TILE, hd), BF16)
                    continue
                used = place + (me ^ j) * share + i * group < held
                old_ref[at, hd:] = jnp.where(used, piece[source, hd:].astype(F32), 0.0).astype(BF16)
                old_ref[at, :hd] = jnp.where(used, 1.0, 0.0).astype(BF16)

        for i in range(most):
            pl.when(i < tiles - 1)(functools.partial(lay, i, True))
            pl.when(i == tiles - 1)(functools.partial(lay, i, False))
        for piece in pieces:
            limit = jnp.maximum(limit, longest(piece[:, :hd]))
        old_limit_ref[...] = limit

    factor = hd ** (-0.5) * math.log2(math.e)
    key_limit = jnp.max(jnp.maximum(old_limit_ref[...], limits_ref[0]))
    small = key_limit * jnp.max(limits_ref[1]) * (1.05 / hd) < SAFE * SAFE

    tile_rows = ROW_TILE * heads

    def queries(t):
        return q_ref[pl.ds(start_row * heads + t * tile_rows, tile_rows), :]

    def old_keys(i):
        source = pl.ds(i * KEY_TILE, KEY_TILE)
        return jnp.concatenate([piece[source, :hd] for piece in pieces], axis=0)

    def new_scores(t):
        known = start_row + t * ROW_TILE
        scores = dot_t(queries(t), kv_ref[pl.ds(0, known + ROW_TILE), :hd])
        to = lax.broadcasted_iota(jnp.int32, (tile_rows, ROW_TILE), 0) % ROW_TILE
        by = lax.broadcasted_iota(jnp.int32, (tile_rows, ROW_TILE), 1)
        last = jnp.where(by <= to, scores[:, known:], MASKED)
        return jnp.concatenate([scores[:, :known], last], axis=1) if known else last

    def new_values(t):
        return new_ref[pl.ds(0, start_row + (t + 1) * ROW_TILE), :]

    def put(t, both):
        sums = both[:, :hd]
        inverse = pl.reciprocal(sums, approx=True)
        inverse = inverse * (2.0 - sums * inverse)
        out = (both[:, hd:] * inverse).astype(BF16)
        for h in range(heads):
            context[pl.ds(t * ROW_TILE, ROW_TILE), h * hd : (h + 1) * hd] = out[
                h * ROW_TILE : (h + 1) * ROW_TILE
            ]

    def fast(used, begin):
        row_tiles = range(begin // ROW_TILE, min(begin + PART_ROWS, rows) // ROW_TILE)
        steps = [(t, i) for t in row_tiles for i in range(used + 1)]

        def score(t, i):
            return new_scores(t) if i == used else dot_t(queries(t), old_keys(i))

        ahead, both = score(*steps[0]), None
        for at, (t, i) in enumerate(steps):
            scores = ahead
            if at + 1 < len(steps):
                ahead = score(*steps[at + 1])
            weights = jnp.exp2(scores * factor).astype(BF16)
            values = new_values(t) if i == used else old_ref[pl.ds(i * group, group), :]
            part = dot(weights, values)
            both = part if i == 0 else both + part
            if i == used:
                put(t, both)

    def exact(t):
        column = lax.broadcasted_iota(jnp.int32, (tile_rows, group), 1)
        within = column % KEY_TILE
        owner = me ^ (column // KEY_TILE)
        place = within // share * block_rows + within % share + owner * share

        def old_scores(i):
            scores = dot_t(queries(t), old_keys(pl.multiple_of(i, 1)))
            return jnp.where(place + i * group < held, scores, MASKED)

        def raise_high(i, carry):
            top = jnp.max(old_scores(i), axis=1, keepdims=True)
            high[...] = jnp.maximum(high[...], top)
            return carry

        def add(i, carry):
            weights = jnp.exp2((old_scores(i) - high[:, :1]) * factor).astype(BF16)
            total[...] += dot(weights, old_ref[pl.ds(pl.multiple_of(i * group, group), group), :])
            return carry

        high[...] = jnp.zeros_like(high) + jnp.max(new_scores(t), axis=1, keepdims=True)
        lax.fori_loop(0, tiles, raise_high, 0)
        weights = jnp.exp2((new_scores(t) - high[:, :1]) * factor).astype(BF16)
        total[...] = dot(weights, new_values(t))
        lax.fori_loop(0, tiles, add, 0)
        put(t, total[...])

    for begin in range(0, rows, PART_ROWS):
        busy = start_row + begin < span
        for used in range(1, most + 1):
            pl.when(busy & small & (tiles == used))(functools.partial(fast, used, begin))

        @pl.when(busy & jnp.logical_not(small))
        def _():
            for t in range(begin // ROW_TILE, min(begin + PART_ROWS, rows) // ROW_TILE):
                exact(t)

        @pl.when(jnp.logical_not(busy))
        def _():
            context[pl.ds(begin, PART_ROWS), :] = jnp.zeros((PART_ROWS, context.shape[1]), BF16)

    load.wait()
    cols = wout.shape[1] // 4
    for k in (3, 1, 2, 0):
        columns = pl.ds(pl.multiple_of((me ^ k) * cols, cols), cols)
        part = dot(context[...], wout[:, columns]).astype(BF16)
        refs = far_refs if k & 1 else near_refs
        if k < 2:
            refs[0][...] = part
            continue
        size = rows // (len(refs) - 1)
        for i, ref in enumerate(refs[1:]):
            ref[...] = part[i * size : (i + 1) * size]


def hand_on_kernel(in_ref, out_ref):
    pass


def finish_kernel(at, plan_ref, tokens_ref, near_ref, got_ref, *refs):
    out_hbm, done, sems = refs[-3:]
    crossed_refs = refs[: sems.shape[0]]
    size = crossed_refs[0].shape[0]
    stores = []
    for i, crossed_ref in enumerate(crossed_refs):
        here = pl.ds(i * size, size)
        there = pl.ds(at + i * size, size)
        kept = near_ref[here, :].astype(F32) + got_ref[here, :].astype(F32)
        total = tokens_ref[there, :].astype(F32) + (kept + crossed_ref[...].astype(F32))
        row = lax.broadcasted_iota(jnp.int32, total.shape, 0) + (at + i * size)
        done[here, :] = jnp.where(row < plan_ref[1], total, 0.0).astype(BF16)
        stores.append(pltpu.make_async_copy(done.at[here], out_hbm.at[there], sems.at[i]))
        stores[-1].start()
    for store in stores:
        store.wait()


def call(
    kernel, out_shape, in_specs, args, flops, mib=MIB, scratch=(), exps=0, name=None, into=None
):
    outs = out_shape if isinstance(out_shape, (list, tuple)) else [out_shape]
    moved = sum(a.size * a.dtype.itemsize for a in list(args) + list(outs))
    return pl.pallas_call(
        kernel,
        out_shape=out_shape,
        in_specs=in_specs,
        out_specs=jax.tree.map(lambda _: VMEM if into is None else HBM, out_shape),
        input_output_aliases=into or {},
        scratch_shapes=list(scratch),
        cost_estimate=pl.CostEstimate(flops=flops, bytes_accessed=moved, transcendentals=exps),
        compiler_params=pltpu.CompilerParams(vmem_limit_bytes=int(mib * 1024 * 1024)),
        name=name,
    )(*args)


def body(
    tokens,
    norm_gain,
    w_query,
    w_keyval,
    w_out,
    span_lens,
    cached_lens,
    old_table,
    new_table,
    old_cache,
):
    tp = lax.axis_size("tp")
    groups, share, width = old_cache.shape
    block_rows = share * tp
    capacity = groups * block_rows
    rows, cols = tokens.shape
    q_cols = w_query.shape[1]
    features = w_query.shape[0]
    hd = width // 2
    most_held = capacity - rows
    piece_rows = most_held // tp

    def swap(x, bit, axis="tp"):
        size = lax.axis_size(axis)
        return lax.ppermute(x, axis, [(i, i ^ bit) for i in range(size)])

    def exchange(x):
        return lax.all_to_all(x, "seq", split_axis=0, concat_axis=0, tiled=True)

    phased = groups == 8
    pair_of_blocks = jax.ShapeDtypeStruct((2, share, width), BF16)

    with jax.named_scope("tokens_gather"):
        across = swap(tokens, 2)
        beside = swap(tokens, 1)

    with jax.named_scope("cache_gather"):
        beside, stored = lax.optimization_barrier((beside, old_cache))
        arrived = exchange(stored).reshape(groups * share, width)
        plan = jnp.concatenate([cached_lens, span_lens, old_table[0], new_table[0]])
        in_span = lax.broadcasted_iota(jnp.int32, (rows, 1), 0) < span_lens[0]
        own = jnp.where(in_span, tokens, jnp.zeros_like(tokens))
        gain = jnp.where(span_lens[0] > 0, norm_gain, 0.0)
        arrived, across, own, gain, plan = lax.optimization_barrier(
            (arrived, across, own, gain, plan)
        )
        ordered = call(
            functools.partial(order_kernel, share),
            jax.ShapeDtypeStruct((piece_rows, width), BF16),
            [SMEM, VMEM],
            (plan, arrived),
            flops=2 * piece_rows * groups * share * width,
            name="order",
        )
        c_across = swap(ordered, 2)
        c_beside = swap(ordered, 1)

    with jax.named_scope("project"):
        corner = swap(across, 1)
        stacked = rows * (q_cols // hd)
        query, keyval, values, limits = call(
            project_kernel,
            [
                jax.ShapeDtypeStruct((stacked, hd), BF16),
                jax.ShapeDtypeStruct((rows, width), BF16),
                jax.ShapeDtypeStruct((rows, width), BF16),
                jax.ShapeDtypeStruct((2, 8, 128), F32),
            ],
            [VMEM] * 5 + [HBM] * 2,
            (
                own,
                beside,
                across,
                corner,
                gain.reshape(tp, 1, cols),
                w_query,
                w_keyval,
            ),
            flops=2 * rows * features * (q_cols + width),
            mib=PROJECT_MIB,
            scratch=[
                pltpu.VMEM((rows, features), BF16),
                pltpu.VMEM(w_query.shape, BF16),
                pltpu.VMEM(w_keyval.shape, BF16),
                pltpu.SemaphoreType.DMA((2 * tp,)),
            ],
            name="project",
        )

    with jax.named_scope("extend"):
        sent = call(
            functools.partial(extend_kernel, share, block_rows),
            [pair_of_blocks] * (groups // 2)
            if phased
            else [jax.ShapeDtypeStruct((groups * share, width), BF16)],
            [SMEM] + [VMEM] * 2,
            (plan, keyval, arrived),
            flops=4 * groups * share * groups * share * width,
            name="extend",
        )
        *sent, c_across = lax.optimization_barrier((*sent, c_across))
        if phased:
            pairs = [swap(x, 2 * k, "seq") if k else x for k, x in enumerate(sent)]
        cached = (ordered, c_beside, c_across, swap(c_across, 1))

    part = rows // CHUNKS
    tile_rows = ROW_TILE * (q_cols // hd)
    old = []
    mixed = None
    for c in range(CHUNKS):
        last = c == CHUNKS - 1
        pieces = 2 if last else 1
        with jax.named_scope("attend"):
            outs = [jax.ShapeDtypeStruct((part, cols), BF16)]
            outs += [jax.ShapeDtypeStruct((part // pieces, cols), BF16)] * pieces
            outs += outs
            if not old:
                outs += [
                    jax.ShapeDtypeStruct((most_held, width), BF16),
                    jax.ShapeDtypeStruct((8, 128), F32),
                ]
            seen = most_held + (c + 1) * part
            sums = list(call(
                functools.partial(attend_kernel, share, block_rows, c * part, part),
                outs,
                [SMEM] + [VMEM] * 8 + [HBM] + [VMEM] * len(old),
                (plan, query, keyval, values, limits, *cached, w_out, *old),
                flops=4 * part * seen * q_cols + 2 * part * q_cols * features,
                exps=part * seen * (q_cols // hd),
                mib=ATTEND_MIB,
                scratch=[
                    pltpu.VMEM((tile_rows, width), F32),
                    pltpu.VMEM((tile_rows, hd), F32),
                    pltpu.VMEM((part, q_cols), BF16),
                    pltpu.VMEM(w_out.shape, BF16),
                    pltpu.SemaphoreType.DMA,
                ],
                name="attend",
            ))
            far0, far1 = sums[0], sums[1 : 1 + pieces]
            near0, near1 = sums[1 + pieces], sums[2 + pieces : 2 + 2 * pieces]
            old = old or sums[2 + 2 * pieces :]
        with jax.named_scope("reduce"):
            if c == 0 and phased:
                far1[0], *pairs = lax.optimization_barrier((far1[0], *pairs))
            got1 = [swap(x, 1) for x in far1]
            if c and last:
                before = pl.pallas_call(
                    hand_on_kernel,
                    out_shape=jax.ShapeDtypeStruct(before.shape, BF16),
                    in_specs=[pl.BlockSpec(memory_space=pl.ANY)],
                    out_specs=pl.BlockSpec(memory_space=pl.ANY),
                    input_output_aliases={0: 0},
                    cost_estimate=pl.CostEstimate(
                        flops=1 << 34, bytes_accessed=1024, transcendentals=0
                    ),
                    compiler_params=pltpu.CompilerParams(vmem_limit_bytes=1 << 20),
                    name="hand_on",
                )(before)
                before, *got1 = lax.optimization_barrier((before, *got1))
            both = [(x.astype(F32) + y.astype(F32)).astype(BF16) for x, y in zip(near1, got1)]
            if not last:
                query, both[0] = lax.optimization_barrier((query, both[0]))
            crossed = [swap(x, 2) for x in both]
            got0 = swap(far0, 1)
        if not last:
            before, unfinished = crossed[0], (near0, got0)
            continue
        for at, near, got, over in ((0, *unfinished, [before]), (part, near0, got0, crossed)):
            with jax.named_scope("finish"):
                mixed = call(
                    functools.partial(finish_kernel, at),
                    jax.ShapeDtypeStruct((rows, cols), BF16),
                    [SMEM] + [VMEM] * (3 + len(over)) + [HBM] * (at > 0),
                    (plan, own, near, got, *over, *([mixed] if at else [])),
                    flops=4 * part * cols,
                    scratch=[
                        pltpu.VMEM((part, cols), BF16),
                        pltpu.SemaphoreType.DMA((len(over),)),
                    ],
                    name="finish",
                    into={4 + len(over): 0} if at else {},
                )

    with jax.named_scope("exchange"):
        if phased:
            *pairs, _ = lax.optimization_barrier((*pairs, both[-1]))
            onward = call(
                collect_kernel,
                jax.ShapeDtypeStruct((groups // 2, share, width), BF16),
                [VMEM] * len(pairs),
                pairs,
                flops=0,
                mib=8,
                name="collect",
            )
            new_cache = call(
                place_kernel,
                jax.ShapeDtypeStruct(old_cache.shape, BF16),
                [VMEM] * (1 + len(pairs)),
                (swap(onward, 1, "seq"), *pairs),
                flops=0,
                mib=8,
                name="place",
            )
        else:
            new_cache = exchange(sent[0].reshape(groups, share, width))
    return (mixed, new_cache)


def solution(mesh):
    in_specs = (
        P("seq", "tp"),
        P(),
        P(None, "tp"),
        P(),
        P("tp", None),
        P("seq"),
        P("seq"),
        P("seq", None),
        P("seq", None),
        P("seq", "tp", None),
    )
    out_specs = (P("seq", "tp"), P("seq", "tp", None))
    return jax.shard_map(body, mesh=mesh, in_specs=in_specs, out_specs=out_specs, check_vma=False)
```

profile of v0, /device:TPU:0, one launch (start us, length us, event | category | flops | bytes accessed | tf_op | source)
XLA Modules:
  0.0 65.7 jit_solution(1471962539987120082)
XLA Ops:
  1.1 2.6 %collective-permute-start.1 = (bf16[512,512]{1,0:T(8,128)(2,1)}, bf16[512,512]{1,0:T(8,128)(2,1)S(1)}, u32[]{:S(2)}, u32[]{:S(2)}) collective-permute-start(bf16[512,512]{1,0:T(8,128)(2,1)} %param.10), channel_id=1, source_target_pairs={{0,2},{1,3},{2,0},{3,1},{4,6},{5,7},{6,4},{7,5},{8,10},{9,11},{10,... | collective-permute-start | bytes 1572872 | tf_op jit(solution)/shard_map/tokens_gather/ppermute | solution.py:373
  5.1 0.8 %pad_add_fusion.plan_ref = s32[18]{0:T(128)S(1)} fusion(s32[8]{0:T(128)} %bitcast.10, s32[8]{0:T(128)} %bitcast.11, s32[1]{0:T(128)} %copy.16, s32[1]{0:T(128)S(6)} %copy.17), kind=kLoop, calls=%fused_computation.6 | loop fusion | flops 54 | bytes 144 | tf_op jit(solution)/shard_map/cache_gather/concatenate | solution.py:388
  5.8 5.8 %all-to-all-start = ((bf16[8,64,256]{2,1,0:T(8,128)(2,1)}), bf16[8,64,256]{2,1,0:T(8,128)(2,1)S(1)}, u32[]{:S(2)}, u32[]{:S(2)}) async-start(bf16[8,64,256]{2,1,0:T(8,128)(2,1)} %param.19), calls=%async_computation | async-start | bytes 524288 | tf_op jit(solution)/shard_map/cache_gather/all_to_all | solution.py:376
  11.6 0.7 %broadcast_select_fusion.1 = f32[2048]{0:T(1024)S(1)} fusion(f32[2048]{0:T(1024)} %param.11, pred[]{:T(512)S(6)} %gt.3), kind=kLoop, calls=%fused_computation.4 | loop fusion | flops 2048 | bytes 16385 | tf_op jit(solution)/shard_map/cache_gather/jit(_where)/select_n | solution.py:391
  12.3 1.2 %broadcast_select_fusion.x0.tokens_ref = bf16[512,512]{1,0:T(8,128)(2,1)S(1)} fusion(bf16[512,512]{1,0:T(8,128)(2,1)} %param.10, pred[512]{0:T(512)(128)(4,1)S(1)} %iota_compare_fusion), kind=kLoop, calls=%fused_computation.1 | loop fusion | flops 262144 | bytes 1049088 | tf_op jit(solution)/shard_map/cache_gather/jit(_where)/select_n | solution.py:390
  13.5 3.0 %collective-permute-done.1.x2 = bf16[512,512]{1,0:T(8,128)(2,1)S(1)} collective-permute-done((bf16[512,512]{1,0:T(8,128)(2,1)}, bf16[512,512]{1,0:T(8,128)(2,1)S(1)}, u32[]{:S(2)}, u32[]{:S(2)}) %collective-permute-start.1) | collective-permute-done | bytes 524320 | tf_op jit(solution)/shard_map/tokens_gather/ppermute | solution.py:373
  16.5 4.4 %all-to-all-done = bf16[8,64,256]{2,1,0:T(8,128)(2,1)S(1)} async-done(((bf16[8,64,256]{2,1,0:T(8,128)(2,1)}), bf16[8,64,256]{2,1,0:T(8,128)(2,1)S(1)}, u32[]{:S(2)}, u32[]{:S(2)}) %all-to-all-start) | async-done | bytes 262176 | tf_op jit(solution)/shard_map/cache_gather/all_to_all | solution.py:376
  20.9 0.8 %order.1.refs_1_ = bf16[384,256]{1,0:T(8,128)(2,1)S(1)} custom-call(s32[18]{0:T(128)S(1)} %pad_add_fusion.plan_ref, bf16[512,256]{1,0:T(8,128)(2,1)S(1)} %bitcast.7), custom_call_target="tpu_custom_call" | custom-call | flops 100663296 | bytes 458824 | tf_op jit(solution)/shard_map/cache_gather/order/pallas_call | solution.py:335
  22.8 4.1 %project.1 = (bf16[2048,128]{1,0:T(8,128)(2,1)S(1)}, bf16[512,256]{1,0:T(8,128)(2,1)S(1)}, bf16[512,256]{1,0:T(8,128)(2,1)S(1)}, f32[2,8,128]{2,1,0:T(8,128)S(1)}) custom-call(bf16[512,512]{1,0:T(8,128)(2,1)S(1)} %broadcast_select_fusion.x0.tokens_ref, bf16[512,512]{1,0:T(8,128)(2,1)S(1)} %collective-permute-done.x1, ...), custom_call_target="tpu_custom_call" | custom-call | flops 1610612736 | bytes 6307840 | tf_op jit(solution)/shard_map/project/project/pallas_call | solution.py:335
  26.9 1.2 %extend.1 = (bf16[2,64,256]{2,1,0:T(8,128)(2,1)S(1)}, bf16[2,64,256]{2,1,0:T(8,128)(2,1)S(1)}, bf16[2,64,256]{2,1,0:T(8,128)(2,1)S(1)}, bf16[2,64,256]{2,1,0:T(8,128)(2,1)S(1)}) custom-call(s32[18]{0:T(128)S(1)} %pad_add_fusion.plan_ref, bf16[512,256]{1,0:T(8,128)(2,1)S(1)} %get-tuple-element.55.kv_ref, bf16[512,256]{1,0:T(8,128)(2,1)S(1)} %bitcast.8), custom_call_target="tpu_custom_call" | custom-call | flops 268435456 | bytes 786504 | tf_op jit(solution)/shard_map/extend/extend/pallas_call | solution.py:335
  28.1 1.0 %collective-permute-done.4.refs_3_ = bf16[384,256]{1,0:T(8,128)(2,1)S(1)} collective-permute-done((bf16[384,256]{1,0:T(8,128)(2,1)S(1)}, bf16[384,256]{1,0:T(8,128)(2,1)S(1)}, u32[]{:S(2)}, u32[]{:S(2)}) %collective-permute-start.4) | collective-permute-done | bytes 196640 | tf_op jit(solution)/shard_map/cache_gather/ppermute | solution.py:373
  29.1 1.1 %collective-permute-start.6 = (bf16[2,64,256]{2,1,0:T(8,128)(2,1)S(1)}, bf16[2,64,256]{2,1,0:T(8,128)(2,1)S(1)}, u32[]{:S(2)}, u32[]{:S(2)}) collective-permute-start(bf16[2,64,256]{2,1,0:T(8,128)(2,1)S(1)} %get-tuple-element.67), channel_id=1, source_target_pairs={{0,8},{4,12},{8,0},{12,4},{16,24},{20,28},{24,16},{28,20},{1,9},{5... | collective-permute-start | bytes 196616 | tf_op jit(solution)/shard_map/extend/ppermute | solution.py:373
  30.8 2.7 %collective-permute-start.8 = (bf16[2,64,256]{2,1,0:T(8,128)(2,1)S(1)}, bf16[2,64,256]{2,1,0:T(8,128)(2,1)S(1)}, u32[]{:S(2)}, u32[]{:S(2)}) collective-permute-start(bf16[2,64,256]{2,1,0:T(8,128)(2,1)S(1)} %get-tuple-element.69), channel_id=1, source_target_pairs={{0,24},{4,28},{8,16},{12,20},{16,8},{20,12},{24,0},{28,4},{1,25},{... | collective-permute-start | bytes 196616 | tf_op jit(solution)/shard_map/extend/ppermute | solution.py:373
  33.5 7.3 %attend.2 = (bf16[256,512]{1,0:T(8,128)(2,1)S(1)}, bf16[256,512]{1,0:T(8,128)(2,1)S(1)}, bf16[256,512]{1,0:T(8,128)(2,1)S(1)}, bf16[256,512]{1,0:T(8,128)(2,1)S(...) custom-call(s32[18]{0:T(128)S(1)} %pad_add_fusion.plan_ref, bf16[2048,128]{1,0:T(8,128)(2,1)S(1)} %get-tuple-element.71.q_ref, ...), custom_call_target="tpu_custom_call" | custom-call | flops 1476395008 | bytes 5779528 | tf_op jit(solution)/shard_map/attend/attend/pallas_call | solution.py:335
  40.9 1.5 %collective-permute-done.9 = bf16[256,512]{1,0:T(8,128)(2,1)S(1)} collective-permute-done((bf16[256,512]{1,0:T(8,128)(2,1)S(1)}, bf16[256,512]{1,0:T(8,128)(2,1)S(1)}, u32[]{:S(2)}, u32[]{:S(2)}) %collective-permute-start.9) | collective-permute-done | bytes 262176 | tf_op jit(solution)/shard_map/reduce/ppermute | solution.py:373
  43.1 7.1 %attend.3 = (bf16[256,512]{1,0:T(8,128)(2,1)S(1)}, bf16[128,512]{1,0:T(8,128)(2,1)S(1)}, bf16[128,512]{1,0:T(8,128)(2,1)S(1)}, bf16[256,512]{1,0:T(8,128)(2,1)S(...) custom-call(s32[18]{0:T(128)S(1)} %pad_add_fusion.plan_ref, ...), custom_call_target="tpu_custom_call" | custom-call | flops 1610612736 | bytes 5779528 | tf_op jit(solution)/shard_map/attend/attend/pallas_call | solution.py:335
  52.2 1.5 %collective-permute-start.15 = (bf16[128,512]{1,0:T(8,128)(2,1)S(1)}, bf16[128,512]{1,0:T(8,128)(2,1)S(1)}, u32[]{:S(2)}, u32[]{:S(2)}) collective-permute-start(bf16[128,512]{1,0:T(8,128)(2,1)S(1)} %add_convert_fusion.1), channel_id=1, source_target_pairs={{0,2},{1,3},{2,0},{3,1},{4,6},{5,7},{6,4},{7,5},{8,10},{9,11},{10,... | collective-permute-start | bytes 393224 | tf_op jit(solution)/shard_map/reduce/ppermute | solution.py:373
  53.8 5.2 %collective-permute-start.17 = (bf16[4,64,256]{2,1,0:T(8,128)(2,1)S(1)}, bf16[4,64,256]{2,1,0:T(8,128)(2,1)S(1)}, u32[]{:S(2)}, u32[]{:S(2)}) collective-permute-start(bf16[4,64,256]{2,1,0:T(8,128)(2,1)S(1)} %collect.1), channel_id=1, source_target_pairs={{0,4},{4,0},{8,12},{12,8},{16,20},{20,16},{24,28},{28,24},{1,5},{5... | collective-permute-start | bytes 393224 | tf_op jit(solution)/shard_map/exchange/ppermute | solution.py:373
  59.0 0.7 %collective-permute-start.14 = (bf16[128,512]{1,0:T(8,128)(2,1)S(1)}, bf16[128,512]{1,0:T(8,128)(2,1)S(1)}, u32[]{:S(2)}, u32[]{:S(2)}) collective-permute-start(bf16[128,512]{1,0:T(8,128)(2,1)S(1)} %add_convert_fusion.2), channel_id=1, source_target_pairs={{0,2},{1,3},{2,0},{3,1},{4,6},{5,7},{6,4},{7,5},{8,10},{9,11},{10,... | collective-permute-start | bytes 393224 | tf_op jit(solution)/shard_map/reduce/ppermute | solution.py:373
  59.7 1.4 %finish.2.refs_2_ = bf16[512,512]{1,0:T(8,128)(2,1)} custom-call(s32[18]{0:T(128)S(1)} %pad_add_fusion.plan_ref, bf16[512,512]{1,0:T(8,128)(2,1)S(1)} %broadcast_select_fusion.x0.tokens_ref, bf16[256,512]{1,0:T(8,128)(2,1)S(1)} %get-tuple-element.83.near_ref, bf16[256,512]{1,0:T(8,128)(2,1)S(1)} %collective-permute-done.16.got_ref, ...), custom_call_target="tpu_custom_call" | custom-call | flops 524288 | bytes 1835080 | tf_op jit(solution)/shard_map/finish/finish/pallas_call | solution.py:335
  61.1 1.5 %collective-permute-done.17.got_ref = bf16[4,64,256]{2,1,0:T(8,128)(2,1)S(1)} collective-permute-done((bf16[4,64,256]{2,1,0:T(8,128)(2,1)S(1)}, bf16[4,64,256]{2,1,0:T(8,128)(2,1)S(1)}, u32[]{:S(2)}, u32[]{:S(2)}) %collective-permute-start.17) | collective-permute-done | bytes 131104 | tf_op jit(solution)/shard_map/exchange/ppermute | solution.py:373
  62.6 0.7 %place.1 = bf16[8,64,256]{2,1,0:T(8,128)(2,1)} custom-call(bf16[4,64,256]{2,1,0:T(8,128)(2,1)S(1)} %collective-permute-done.17.got_ref, bf16[2,64,256]{2,1,0:T(8,128)(2,1)S(1)} %get-tuple-element.90.refs_0_, bf16[2,64,256]{2,1,0:T(8,128)(2,1)S(1)} %collective-permute-done.6.refs_1_, bf16[2,64,256]{2,1,0:T(8,128)(2,1)S(1)} %collective-permute-done.7.refs_2_, ...), custom_call_target="tpu_custom_call" | custom-call | bytes 655360 | tf_op jit(solution)/shard_map/exchange/place/pallas_call | solution.py:335
  63.3 0.8 %collective-permute-done.14.refs_0_ = bf16[128,512]{1,0:T(8,128)(2,1)S(1)} collective-permute-done((bf16[128,512]{1,0:T(8,128)(2,1)S(1)}, bf16[128,512]{1,0:T(8,128)(2,1)S(1)}, u32[]{:S(2)}, u32[]{:S(2)}) %collective-permute-start.14) | collective-permute-done | bytes 131104 | tf_op jit(solution)/shard_map/reduce/ppermute | solution.py:373
  64.1 1.4 %finish.3 = bf16[512,512]{1,0:T(8,128)(2,1)} custom-call(s32[18]{0:T(128)S(1)} %pad_add_fusion.plan_ref, bf16[512,512]{1,0:T(8,128)(2,1)S(1)} %broadcast_select_fusion.x0.tokens_ref, bf16[256,512]{1,0:T(8,128)(2,1)S(1)} %get-tuple-element.74.near_ref, bf16[256,512]{1,0:T(8,128)(2,1)S(1)} %collective-permute-done.10.got_ref, ...), custom_call_target="tpu_custom_call", output_to_operand_aliasing={{}: (6, {})} | custom-call | flops 524288 | bytes 2359368 | tf_op jit(solution)/shard_map/finish/finish/pallas_call | solution.py:335
  (31 shorter events, 5.1 us)
Async XLA Ops:
  0.6 5.2 %collective-permute-start = (bf16[512,512]{1,0:T(8,128)(2,1)}, bf16[512,512]{1,0:T(8,128)(2,1)S(1)}, u32[]{:S(2)}, u32[]{:S(2)}) collective-permute-start(bf16[512,512]{1,0:T(8,128)(2,1)} %param.10), channel_id=1, source_target_pairs={{0,1},{1,0},{2,3},{3,2},{4,5},{5,4},{6,7},{7,6},{8,9},{9,8},{10,11... | collective-permute-start | bytes 1572872 | tf_op jit(solution)/shard_map/tokens_gather/ppermute | solution.py:373
  1.1 15.3 %collective-permute-start.1 = (bf16[512,512]{1,0:T(8,128)(2,1)}, bf16[512,512]{1,0:T(8,128)(2,1)S(1)}, u32[]{:S(2)}, u32[]{:S(2)}) collective-permute-start(bf16[512,512]{1,0:T(8,128)(2,1)} %param.10), channel_id=1, source_target_pairs={{0,2},{1,3},{2,0},{3,1},{4,6},{5,7},{6,4},{7,5},{8,10},{9,11},{10,... | collective-permute-start | bytes 1572872 | tf_op jit(solution)/shard_map/tokens_gather/ppermute | solution.py:373
  5.8 15.1 %all-to-all-start = ((bf16[8,64,256]{2,1,0:T(8,128)(2,1)}), bf16[8,64,256]{2,1,0:T(8,128)(2,1)S(1)}, u32[]{:S(2)}, u32[]{:S(2)}) async-start(bf16[8,64,256]{2,1,0:T(8,128)(2,1)} %param.19), calls=%async_computation | async-start | bytes 524288 | tf_op jit(solution)/shard_map/cache_gather/all_to_all | solution.py:376
  20.9 1.9 %collective-permute-start.2 = (bf16[512,512]{1,0:T(8,128)(2,1)S(1)}, bf16[512,512]{1,0:T(8,128)(2,1)S(1)}, u32[]{:S(2)}, u32[]{:S(2)}) collective-permute-start(bf16[512,512]{1,0:T(8,128)(2,1)S(1)} %collective-permute-done.1.x2), channel_id=1, source_target_pairs={{0,1},{1,0},{2,3},{3,2},{4,5},{5,4},{6,7},{7,6},{8,9},{9,8},{10,11... | collective-permute-start | bytes 1572872 | tf_op jit(solution)/shard_map/project/ppermute | solution.py:373
  21.7 7.4 %collective-permute-start.4 = (bf16[384,256]{1,0:T(8,128)(2,1)S(1)}, bf16[384,256]{1,0:T(8,128)(2,1)S(1)}, u32[]{:S(2)}, u32[]{:S(2)}) collective-permute-start(bf16[384,256]{1,0:T(8,128)(2,1)S(1)} %order.1.refs_1_), channel_id=1, source_target_pairs={{0,2},{1,3},{2,0},{3,1},{4,6},{5,7},{6,4},{7,5},{8,10},{9,11},{10,... | collective-permute-start | bytes 589832 | tf_op jit(solution)/shard_map/cache_gather/ppermute | solution.py:373
  22.2 11.2 %collective-permute-start.3 = (bf16[384,256]{1,0:T(8,128)(2,1)S(1)}, bf16[384,256]{1,0:T(8,128)(2,1)S(1)}, u32[]{:S(2)}, u32[]{:S(2)}) collective-permute-start(bf16[384,256]{1,0:T(8,128)(2,1)S(1)} %order.1.refs_1_), channel_id=1, source_target_pairs={{0,1},{1,0},{2,3},{3,2},{4,5},{5,4},{6,7},{7,6},{8,9},{9,8},{10,11... | collective-permute-start | bytes 589832 | tf_op jit(solution)/shard_map/cache_gather/ppermute | solution.py:373
  29.1 4.4 %collective-permute-start.5 = (bf16[384,256]{1,0:T(8,128)(2,1)S(1)}, bf16[384,256]{1,0:T(8,128)(2,1)S(1)}, u32[]{:S(2)}, u32[]{:S(2)}) collective-permute-start(bf16[384,256]{1,0:T(8,128)(2,1)S(1)} %collective-permute-done.4.refs_3_), channel_id=1, source_target_pairs={{0,1},{1,0},{2,3},{3,2},{4,5},{5,4},{6,7},{7,6},{8,9},{9,8},{10,11... | collective-permute-start | bytes 589832 | tf_op jit(solution)/shard_map/extend/ppermute | solution.py:373
  29.1 11.7 %collective-permute-start.6 = (bf16[2,64,256]{2,1,0:T(8,128)(2,1)S(1)}, bf16[2,64,256]{2,1,0:T(8,128)(2,1)S(1)}, u32[]{:S(2)}, u32[]{:S(2)}) collective-permute-start(bf16[2,64,256]{2,1,0:T(8,128)(2,1)S(1)} %get-tuple-element.67), channel_id=1, source_target_pairs={{0,8},{4,12},{8,0},{12,4},{16,24},{20,28},{24,16},{28,20},{1,9},{5... | collective-permute-start | bytes 196616 | tf_op jit(solution)/shard_map/extend/ppermute | solution.py:373
  30.1 10.7 %collective-permute-start.7 = (bf16[2,64,256]{2,1,0:T(8,128)(2,1)S(1)}, bf16[2,64,256]{2,1,0:T(8,128)(2,1)S(1)}, u32[]{:S(2)}, u32[]{:S(2)}) collective-permute-start(bf16[2,64,256]{2,1,0:T(8,128)(2,1)S(1)} %get-tuple-element.68), channel_id=1, source_target_pairs={{0,16},{4,20},{8,24},{12,28},{16,0},{20,4},{24,8},{28,12},{1,17},{... | collective-permute-start | bytes 196616 | tf_op jit(solution)/shard_map/extend/ppermute | solution.py:373
  30.8 10.0 %collective-permute-start.8 = (bf16[2,64,256]{2,1,0:T(8,128)(2,1)S(1)}, bf16[2,64,256]{2,1,0:T(8,128)(2,1)S(1)}, u32[]{:S(2)}, u32[]{:S(2)}) collective-permute-start(bf16[2,64,256]{2,1,0:T(8,128)(2,1)S(1)} %get-tuple-element.69), channel_id=1, source_target_pairs={{0,24},{4,28},{8,16},{12,20},{16,8},{20,12},{24,0},{28,4},{1,25},{... | collective-permute-start | bytes 196616 | tf_op jit(solution)/shard_map/extend/ppermute | solution.py:373
  40.8 1.6 %collective-permute-start.9 = (bf16[256,512]{1,0:T(8,128)(2,1)S(1)}, bf16[256,512]{1,0:T(8,128)(2,1)S(1)}, u32[]{:S(2)}, u32[]{:S(2)}) collective-permute-start(bf16[256,512]{1,0:T(8,128)(2,1)S(1)} %get-tuple-element.70), channel_id=1, source_target_pairs={{0,1},{1,0},{2,3},{3,2},{4,5},{5,4},{6,7},{7,6},{8,9},{9,8},{10,11... | collective-permute-start | bytes 786440 | tf_op jit(solution)/shard_map/reduce/ppermute | solution.py:373
  42.5 8.9 %collective-permute-start.11 = (bf16[256,512]{1,0:T(8,128)(2,1)S(1)}, bf16[256,512]{1,0:T(8,128)(2,1)S(1)}, u32[]{:S(2)}, u32[]{:S(2)}) collective-permute-start(bf16[256,512]{1,0:T(8,128)(2,1)S(1)} %add_convert_fusion), channel_id=1, source_target_pairs={{0,2},{1,3},{2,0},{3,1},{4,6},{5,7},{6,4},{7,5},{8,10},{9,11},{10,... | collective-permute-start | bytes 786440 | tf_op jit(solution)/shard_map/reduce/ppermute | solution.py:373
  43.1 16.6 %collective-permute-start.16 = (bf16[256,512]{1,0:T(8,128)(2,1)S(1)}, bf16[256,512]{1,0:T(8,128)(2,1)S(1)}, u32[]{:S(2)}, u32[]{:S(2)}) collective-permute-start(bf16[256,512]{1,0:T(8,128)(2,1)S(1)} %get-tuple-element.84), channel_id=1, source_target_pairs={{0,1},{1,0},{2,3},{3,2},{4,5},{5,4},{6,7},{7,6},{8,9},{9,8},{10,11... | collective-permute-start | bytes 786440 | tf_op jit(solution)/shard_map/reduce/ppermute | solution.py:373
  50.3 1.6 %collective-permute-start.12 = (bf16[128,512]{1,0:T(8,128)(2,1)S(1)}, bf16[128,512]{1,0:T(8,128)(2,1)S(1)}, u32[]{:S(2)}, u32[]{:S(2)}) collective-permute-start(bf16[128,512]{1,0:T(8,128)(2,1)S(1)} %get-tuple-element.78), channel_id=1, source_target_pairs={{0,1},{1,0},{2,3},{3,2},{4,5},{5,4},{6,7},{7,6},{8,9},{9,8},{10,11... | collective-permute-start | bytes 393224 | tf_op jit(solution)/shard_map/reduce/ppermute | solution.py:373
  50.8 1.3 %collective-permute-start.13 = (bf16[128,512]{1,0:T(8,128)(2,1)S(1)}, bf16[128,512]{1,0:T(8,128)(2,1)S(1)}, u32[]{:S(2)}, u32[]{:S(2)}) collective-permute-start(bf16[128,512]{1,0:T(8,128)(2,1)S(1)} %get-tuple-element.79), channel_id=1, source_target_pairs={{0,1},{1,0},{2,3},{3,2},{4,5},{5,4},{6,7},{7,6},{8,9},{9,8},{10,11... | collective-permute-start | bytes 393224 | tf_op jit(solution)/shard_map/reduce/ppermute | solution.py:373
  50.9 12.4 %collective-permute-start.10 = (bf16[256,512]{1,0:T(8,128)(2,1)S(1)}, bf16[256,512]{1,0:T(8,128)(2,1)S(1)}, u32[]{:S(2)}, u32[]{:S(2)}) collective-permute-start(bf16[256,512]{1,0:T(8,128)(2,1)S(1)} %get-tuple-element.75), channel_id=1, source_target_pairs={{0,1},{1,0},{2,3},{3,2},{4,5},{5,4},{6,7},{7,6},{8,9},{9,8},{10,11... | collective-permute-start | bytes 786440 | tf_op jit(solution)/shard_map/reduce/ppermute | solution.py:373
  52.2 11.1 %collective-permute-start.15 = (bf16[128,512]{1,0:T(8,128)(2,1)S(1)}, bf16[128,512]{1,0:T(8,128)(2,1)S(1)}, u32[]{:S(2)}, u32[]{:S(2)}) collective-permute-start(bf16[128,512]{1,0:T(8,128)(2,1)S(1)} %add_convert_fusion.1), channel_id=1, source_target_pairs={{0,2},{1,3},{2,0},{3,1},{4,6},{5,7},{6,4},{7,5},{8,10},{9,11},{10,... | collective-permute-start | bytes 393224 | tf_op jit(solution)/shard_map/reduce/ppermute | solution.py:373
  53.8 8.8 %collective-permute-start.17 = (bf16[4,64,256]{2,1,0:T(8,128)(2,1)S(1)}, bf16[4,64,256]{2,1,0:T(8,128)(2,1)S(1)}, u32[]{:S(2)}, u32[]{:S(2)}) collective-permute-start(bf16[4,64,256]{2,1,0:T(8,128)(2,1)S(1)} %collect.1), channel_id=1, source_target_pairs={{0,4},{4,0},{8,12},{12,8},{16,20},{20,16},{24,28},{28,24},{1,5},{5... | collective-permute-start | bytes 393224 | tf_op jit(solution)/shard_map/exchange/ppermute | solution.py:373
  59.0 5.1 %collective-permute-start.14 = (bf16[128,512]{1,0:T(8,128)(2,1)S(1)}, bf16[128,512]{1,0:T(8,128)(2,1)S(1)}, u32[]{:S(2)}, u32[]{:S(2)}) collective-permute-start(bf16[128,512]{1,0:T(8,128)(2,1)S(1)} %add_convert_fusion.2), channel_id=1, source_target_pairs={{0,2},{1,3},{2,0},{3,1},{4,6},{5,7},{6,4},{7,5},{8,10},{9,11},{10,... | collective-permute-start | bytes 393224 | tf_op jit(solution)/shard_map/reduce/ppermute | solution.py:373
where the time goes:
time: 64.7 us; the launch traced here: 65.7 us
  Pallas kernels  24 us (37%)
  starting transfers between devices  23.4 us (36%)
  waiting for transfers between devices  13.3 us (21%)
  other arithmetic  2.77 us (4%)
  between operations  2.21 us (3%)
    pallas_call x9, Pallas kernels, call(): pl.pallas_call(kernel, out_shape=out_shape, in_specs=in_specs, out_specs=...  24 us
    ppermute x18, starting transfers between devices, swap(): return lax.ppermute(x, axis, [(i, i ^ bit) for i in range(size)])  17.5 us
    ppermute x18, waiting for transfers between devices, swap(): return lax.ppermute(x, axis, [(i, i ^ bit) for i in range(size)])  8.92 us
    all_to_all x1, starting transfers between devices, exchange(): return lax.all_to_all(x, 'seq', split_axis=0, concat_axis=0, tiled=True)  5.81 us
    all_to_all x1, waiting for transfers between devices, exchange(): return lax.all_to_all(x, 'seq', split_axis=0, concat_axis=0, tiled=True)  4.39 us
  transfers between devices with their start and end apart: 19, of which 9 were waited for; matrix products, arithmetic and copies ran while one was open for 4% of the time, Pallas kernels for 34%

commit v1 on v0

--- a/solution.py
+++ b/solution.py
@@ -17,6 +17,7 @@
 NORM_ROWS = 128
 MIB = 51
 PROJECT_MIB = 50.375
+LEAST = -3e38
 ATTEND_MIB = 49.75
 SAFE = 60.0
 F32 = jnp.float32
@@ -35,16 +36,17 @@
     return lax.dot_general(a, b, (((1,), (1,)), ((), ())), preferred_element_type=F32)
 
 
-def collect_kernel(*refs):
-    for k, pair_ref in enumerate(refs[:-1]):
-        refs[-1][k] = pair_ref[1]
-
-
-def place_kernel(got_ref, *refs):
+def pair_kernel(keep_ref, got_ref, *pair_refs):
+    for k, pair_ref in enumerate(pair_refs):
+        pair_ref[0] = keep_ref[k]
+        pair_ref[1] = got_ref[k]
+
+
+def place_kernel(*refs):
     me = lax.axis_index("seq")
     for k, pair_ref in enumerate(refs[:-1]):
-        refs[-1][me ^ (2 * k)] = pair_ref[0]
-        refs[-1][me ^ (2 * k + 1)] = got_ref[k]
+        for j in range(2):
+            refs[-1][me ^ (2 * k + j)] = pair_ref[j]
 
 
 def order_kernel(share, plan_ref, arrived_ref, out_ref):
@@ -85,7 +87,7 @@
         out_refs[0][...] = total
         return
     for slot in range(groups):
-        out_refs[slot // 2][slot % 2] = total[slot * share : (slot + 1) * share]
+        out_refs[slot % 2][slot // 2] = total[slot * share : (slot + 1) * share]
 
 
 def project_kernel(
@@ -160,8 +162,7 @@
         old_ref, old_limit_ref = refs[10:12]
     total, high, context, wout, sem = refs[-5:]
     at = 8 if start_row else 6
-    count = (len(refs) - 5 - at) // 2 if start_row else 2
-    far_refs, near_refs = refs[at : at + count], refs[at + count : at + 2 * count]
+    far_refs, near_refs = refs[at : at + 2], refs[at + 2 : at + 4]
     me = lax.axis_index("tp")
     held, span = plan_ref[0], plan_ref[1]
     piece_rows, width = pieces[0].shape
@@ -296,30 +297,26 @@
     for k in (3, 1, 2, 0):
         columns = pl.ds(pl.multiple_of((me ^ k) * cols, cols), cols)
         part = dot(context[...], wout[:, columns]).astype(BF16)
-        refs = far_refs if k & 1 else near_refs
-        if k < 2:
-            refs[0][...] = part
-            continue
-        size = rows // (len(refs) - 1)
-        for i, ref in enumerate(refs[1:]):
-            ref[...] = part[i * size : (i + 1) * size]
+        if k & 1:
+            far_refs[k >> 1][...] = part
+        else:
+            near_refs[k >> 1][...] = part
 
 
 def hand_on_kernel(in_ref, out_ref):
     pass
 
 
-def finish_kernel(at, plan_ref, tokens_ref, near_ref, got_ref, *refs):
+def finish_kernel(at, plan_ref, tokens_ref, near_ref, got_ref, crossed_ref, *refs):
     out_hbm, done, sems = refs[-3:]
-    crossed_refs = refs[: sems.shape[0]]
-    size = crossed_refs[0].shape[0]
+    half = near_ref.shape[0] // 2
     stores = []
-    for i, crossed_ref in enumerate(crossed_refs):
-        here = pl.ds(i * size, size)
-        there = pl.ds(at + i * size, size)
+    for i in range(2):
+        here = pl.ds(i * half, half)
+        there = pl.ds(at + i * half, half)
         kept = near_ref[here, :].astype(F32) + got_ref[here, :].astype(F32)
-        total = tokens_ref[there, :].astype(F32) + (kept + crossed_ref[...].astype(F32))
-        row = lax.broadcasted_iota(jnp.int32, total.shape, 0) + (at + i * size)
+        total = tokens_ref[there, :].astype(F32) + (kept + crossed_ref[here, :].astype(F32))
+        row = lax.broadcasted_iota(jnp.int32, total.shape, 0) + (at + i * half)
         done[here, :] = jnp.where(row < plan_ref[1], total, 0.0).astype(BF16)
         stores.append(pltpu.make_async_copy(done.at[here], out_hbm.at[there], sems.at[i]))
         stores[-1].start()
@@ -376,7 +373,6 @@
         return lax.all_to_all(x, "seq", split_axis=0, concat_axis=0, tiled=True)
 
     phased = groups == 8
-    pair_of_blocks = jax.ShapeDtypeStruct((2, share, width), BF16)
 
     with jax.named_scope("tokens_gather"):
         across = swap(tokens, 2)
@@ -385,10 +381,12 @@
     with jax.named_scope("cache_gather"):
         beside, stored = lax.optimization_barrier((beside, old_cache))
         arrived = exchange(stored).reshape(groups * share, width)
-        plan = jnp.concatenate([cached_lens, span_lens, old_table[0], new_table[0]])
-        in_span = lax.broadcasted_iota(jnp.int32, (rows, 1), 0) < span_lens[0]
-        own = jnp.where(in_span, tokens, jnp.zeros_like(tokens))
-        gain = jnp.where(span_lens[0] > 0, norm_gain, 0.0)
+        gain = jnp.maximum(norm_gain, LEAST).reshape(tp, 1, cols)
+        own = jnp.maximum(tokens, jnp.asarray(LEAST, BF16))
+        across, *lens = lax.optimization_barrier(
+            (across, cached_lens, span_lens, old_table[0], new_table[0])
+        )
+        plan = jnp.concatenate(lens)
         arrived, across, own, gain, plan = lax.optimization_barrier(
             (arrived, across, own, gain, plan)
         )
@@ -420,7 +418,7 @@
                 beside,
                 across,
                 corner,
-                gain.reshape(tp, 1, cols),
+                gain,
                 w_query,
                 w_keyval,
             ),
@@ -438,7 +436,7 @@
     with jax.named_scope("extend"):
         sent = call(
             functools.partial(extend_kernel, share, block_rows),
-            [pair_of_blocks] * (groups // 2)
+            [jax.ShapeDtypeStruct((groups // 2, share, width), BF16)] * 2
             if phased
             else [jax.ShapeDtypeStruct((groups * share, width), BF16)],
             [SMEM] + [VMEM] * 2,
@@ -448,7 +446,7 @@
         )
         *sent, c_across = lax.optimization_barrier((*sent, c_across))
         if phased:
-            pairs = [swap(x, 2 * k, "seq") if k else x for k, x in enumerate(sent)]
+            keep, got = sent[0], swap(sent[1], 1, "seq")
         cached = (ordered, c_beside, c_across, swap(c_across, 1))
 
     part = rows // CHUNKS
@@ -457,11 +455,9 @@
     mixed = None
     for c in range(CHUNKS):
         last = c == CHUNKS - 1
-        pieces = 2 if last else 1
         with jax.named_scope("attend"):
             outs = [jax.ShapeDtypeStruct((part, cols), BF16)]
-            outs += [jax.ShapeDtypeStruct((part // pieces, cols), BF16)] * pieces
-            outs += outs
+            outs *= 4
             if not old:
                 outs += [
                     jax.ShapeDtypeStruct((most_held, width), BF16),
@@ -485,13 +481,12 @@
                 ],
                 name="attend",
             ))
-            far0, far1 = sums[0], sums[1 : 1 + pieces]
-            near0, near1 = sums[1 + pieces], sums[2 + pieces : 2 + 2 * pieces]
-            old = old or sums[2 + 2 * pieces :]
+            far0, far1, near0, near1 = sums[:4]
+            old = old or sums[4:]
         with jax.named_scope("reduce"):
             if c == 0 and phased:
-                far1[0], *pairs = lax.optimization_barrier((far1[0], *pairs))
-            got1 = [swap(x, 1) for x in far1]
+                far1, got = lax.optimization_barrier((far1, got))
+            got1 = swap(far1, 1)
             if c and last:
                 before = pl.pallas_call(
                     hand_on_kernel,
@@ -505,48 +500,49 @@
                     compiler_params=pltpu.CompilerParams(vmem_limit_bytes=1 << 20),
                     name="hand_on",
                 )(before)
-                before, *got1 = lax.optimization_barrier((before, *got1))
-            both = [(x.astype(F32) + y.astype(F32)).astype(BF16) for x, y in zip(near1, got1)]
+                before, got1 = lax.optimization_barrier((before, got1))
+            pair = (near1.astype(F32) + got1.astype(F32)).astype(BF16)
             if not last:
-                query, both[0] = lax.optimization_barrier((query, both[0]))
-            crossed = [swap(x, 2) for x in both]
+                query, pair = lax.optimization_barrier((query, pair))
+            if last and phased:
+                pair, got = lax.optimization_barrier((pair, got))
+            crossed = swap(pair, 2)
             got0 = swap(far0, 1)
         if not last:
-            before, unfinished = crossed[0], (near0, got0)
+            before, unfinished = crossed, (near0, got0)
             continue
-        for at, near, got, over in ((0, *unfinished, [before]), (part, near0, got0, crossed)):
+        for at, near, beside, over in ((0, *unfinished, before), (part, near0, got0, crossed)):
             with jax.named_scope("finish"):
                 mixed = call(
                     functools.partial(finish_kernel, at),
                     jax.ShapeDtypeStruct((rows, cols), BF16),
-                    [SMEM] + [VMEM] * (3 + len(over)) + [HBM] * (at > 0),
-                    (plan, own, near, got, *over, *([mixed] if at else [])),
+                    [SMEM] + [VMEM] * 4 + [HBM] * (at > 0),
+                    (plan, own, near, beside, over, *([mixed] if at else [])),
                     flops=4 * part * cols,
                     scratch=[
                         pltpu.VMEM((part, cols), BF16),
-                        pltpu.SemaphoreType.DMA((len(over),)),
+                        pltpu.SemaphoreType.DMA((2,)),
                     ],
                     name="finish",
-                    into={4 + len(over): 0} if at else {},
+                    into={5: 0} if at else {},
                 )
 
     with jax.named_scope("exchange"):
         if phased:
-            *pairs, _ = lax.optimization_barrier((*pairs, both[-1]))
-            onward = call(
-                collect_kernel,
-                jax.ShapeDtypeStruct((groups // 2, share, width), BF16),
-                [VMEM] * len(pairs),
-                pairs,
+            pairs = call(
+                pair_kernel,
+                [jax.ShapeDtypeStruct((2, share, width), BF16)] * (groups // 2),
+                [VMEM] * 2,
+                (keep, got),
                 flops=0,
                 mib=8,
-                name="collect",
+                name="pair",
             )
             new_cache = call(
                 place_kernel,
                 jax.ShapeDtypeStruct(old_cache.shape, BF16),
-                [VMEM] * (1 + len(pairs)),
-                (swap(onward, 1, "seq"), *pairs),
+                [VMEM] * len(pairs),
+                [swap(x, 2 * k, "seq") if k else x for k, x in enumerate(pairs)],
                 flops=0,
                 mib=8,
                 name="place",

time: 64.7 us -> 63.8 us (0.986); the launches traced: 65.7 us -> 64 us
  waiting for transfers between devices: 13.3 us -> 12.2 us
    all_to_all x1, waiting for transfers between devices: 4.39 us -> 2.07 us  [exchange(): return lax.all_to_all(x, 'seq', split_axis=0, concat_axis=0, tiled=True)]
    select_n x2 -> x0, other arithmetic: 1.87 us -> none  [the longest x1 1.17 us: body(): own = jnp.where(in_span, tokens, jnp.zeros_like(tokens))]
    max x0 -> x2, other arithmetic: none -> 1.79 us  [the longest x1 1.09 us: body(): own = jnp.maximum(tokens, jnp.asarray(LEAST, BF16))]
    ppermute x18 -> x16, waiting for transfers between devices: 8.92 us -> 10.1 us  [swap(): return lax.ppermute(x, axis, [(i, i ^ bit) for i in range(size)])]
    ppermute x18 -> x16, starting transfers between devices: 17.5 us -> 16.7 us  [swap(): return lax.ppermute(x, axis, [(i, i ^ bit) for i in range(size)])]
  transfers between devices with their start and end apart: 19 -> 17, of which waited for: 9 -> 6; matrix products, arithmetic and copies ran while one was open for 4% -> 4% of each run, Pallas kernels for 34% -> 35%
where the time goes in v1:
time: 63.8 us; the launch traced here: 64 us
  Pallas kernels  23.9 us (37%)
  starting transfers between devices  23.1 us (36%)
  waiting for transfers between devices  12.2 us (19%)
  other arithmetic  2.67 us (4%)
  between operations  2.18 us (3%)
    pallas_call x9, Pallas kernels, call(): pl.pallas_call(kernel, out_shape=out_shape, in_specs=in_specs, out_specs=...  23.9 us
    ppermute x16, starting transfers between devices, swap(): return lax.ppermute(x, axis, [(i, i ^ bit) for i in range(size)])  16.7 us
    ppermute x16, waiting for transfers between devices, swap(): return lax.ppermute(x, axis, [(i, i ^ bit) for i in range(size)])  10.1 us
    all_to_all x1, starting transfers between devices, exchange(): return lax.all_to_all(x, 'seq', split_axis=0, concat_axis=0, tiled=True)  6.32 us
    all_to_all x1, waiting for transfers between devices, exchange(): return lax.all_to_all(x, 'seq', split_axis=0, concat_axis=0, tiled=True)  2.07 us
  transfers between devices with their start and end apart: 17, of which 6 were waited for; matrix products, arithmetic and copies ran while one was open for 4% of the time, Pallas kernels for 35%

profile of v1, /device:TPU:0, one launch (start us, length us, event | category | flops | bytes accessed | tf_op | source)
XLA Modules:
  0.0 64.0 jit_solution(12910736348756528031)
XLA Ops:
  1.1 2.6 %collective-permute-start.1 = (bf16[512,512]{1,0:T(8,128)(2,1)}, bf16[512,512]{1,0:T(8,128)(2,1)S(1)}, u32[]{:S(2)}, u32[]{:S(2)}) collective-permute-start(bf16[512,512]{1,0:T(8,128)(2,1)} %param.10), channel_id=1, source_target_pairs={{0,2},{1,3},{2,0},{3,1},{4,6},{5,7},{6,4},{7,5},{8,10},{9,11},{10,... | collective-permute-start | bytes 1572872 | tf_op jit(solution)/shard_map/tokens_gather/ppermute | solution.py:370
  3.7 6.3 %all-to-all-start = ((bf16[8,64,256]{2,1,0:T(8,128)(2,1)}), bf16[8,64,256]{2,1,0:T(8,128)(2,1)S(1)}, u32[]{:S(2)}, u32[]{:S(2)}) async-start(bf16[8,64,256]{2,1,0:T(8,128)(2,1)} %param.19), calls=%async_computation | async-start | bytes 524288 | tf_op jit(solution)/shard_map/cache_gather/all_to_all | solution.py:373
  10.1 0.7 %broadcast_maximum_fusion.1 = f32[2048]{0:T(1024)S(1)} fusion(f32[2048]{0:T(1024)} %param.11), kind=kLoop, calls=%fused_computation.3 | loop fusion | flops 2048 | bytes 16384 | tf_op jit(solution)/shard_map/cache_gather/max | solution.py:384
  12.1 1.1 %broadcast_maximum_fusion.x0.tokens_ref = bf16[512,512]{1,0:T(8,128)(2,1)S(1)} fusion(bf16[512,512]{1,0:T(8,128)(2,1)} %param.10), kind=kLoop, calls=%fused_computation.2 | loop fusion | flops 262144 | bytes 1048576 | tf_op jit(solution)/shard_map/cache_gather/max | solution.py:385
  13.2 3.3 %collective-permute-done.1.x2 = bf16[512,512]{1,0:T(8,128)(2,1)S(1)} collective-permute-done((bf16[512,512]{1,0:T(8,128)(2,1)}, bf16[512,512]{1,0:T(8,128)(2,1)S(1)}, u32[]{:S(2)}, u32[]{:S(2)}) %collective-permute-start.1) | collective-permute-done | bytes 524320 | tf_op jit(solution)/shard_map/tokens_gather/ppermute | solution.py:370
  16.5 0.7 %pad_add_fusion.plan_ref = s32[18]{0:T(128)S(1)} fusion(s32[8]{0:T(128)} %bitcast.7, s32[8]{0:T(128)} %bitcast.8, s32[1]{0:T(128)S(6)} %copy.16, s32[1]{0:T(128)S(6)} %copy.17), kind=kLoop, calls=%fused_computation.4 | loop fusion | flops 54 | bytes 144 | tf_op jit(solution)/shard_map/cache_gather/concatenate | solution.py:389
  17.2 2.1 %all-to-all-done = bf16[8,64,256]{2,1,0:T(8,128)(2,1)S(1)} async-done(((bf16[8,64,256]{2,1,0:T(8,128)(2,1)}), bf16[8,64,256]{2,1,0:T(8,128)(2,1)S(1)}, u32[]{:S(2)}, u32[]{:S(2)}) %all-to-all-start) | async-done | bytes 262176 | tf_op jit(solution)/shard_map/cache_gather/all_to_all | solution.py:373
  19.3 0.8 %order.1.refs_1_ = bf16[384,256]{1,0:T(8,128)(2,1)S(1)} custom-call(s32[18]{0:T(128)S(1)} %pad_add_fusion.plan_ref, bf16[512,256]{1,0:T(8,128)(2,1)S(1)} %bitcast.4), custom_call_target="tpu_custom_call" | custom-call | flops 100663296 | bytes 458824 | tf_op jit(solution)/shard_map/cache_gather/order/pallas_call | solution.py:332
  20.1 1.6 %collective-permute-start.4 = (bf16[384,256]{1,0:T(8,128)(2,1)S(1)}, bf16[384,256]{1,0:T(8,128)(2,1)S(1)}, u32[]{:S(2)}, u32[]{:S(2)}) collective-permute-start(bf16[384,256]{1,0:T(8,128)(2,1)S(1)} %order.1.refs_1_), channel_id=1, source_target_pairs={{0,2},{1,3},{2,0},{3,1},{4,6},{5,7},{6,4},{7,5},{8,10},{9,11},{10,... | collective-permute-start | bytes 589832 | tf_op jit(solution)/shard_map/cache_gather/ppermute | solution.py:370
  21.9 4.1 %project.1 = (bf16[2048,128]{1,0:T(8,128)(2,1)S(1)}, bf16[512,256]{1,0:T(8,128)(2,1)S(1)}, bf16[512,256]{1,0:T(8,128)(2,1)S(1)}, f32[2,8,128]{2,1,0:T(8,128)S(1)}) custom-call(bf16[512,512]{1,0:T(8,128)(2,1)S(1)} %broadcast_maximum_fusion.x0.tokens_ref, bf16[512,512]{1,0:T(8,128)(2,1)S(1)} %collective-permute-done.x1, ...), custom_call_target="tpu_custom_call" | custom-call | flops 1610612736 | bytes 6307840 | tf_op jit(solution)/shard_map/project/project/pallas_call | solution.py:332
  26.0 1.2 %extend.1 = (bf16[4,64,256]{2,1,0:T(8,128)(2,1)S(1)}, bf16[4,64,256]{2,1,0:T(8,128)(2,1)S(1)}) custom-call(s32[18]{0:T(128)S(1)} %pad_add_fusion.plan_ref, bf16[512,256]{1,0:T(8,128)(2,1)S(1)} %get-tuple-element.57.kv_ref, bf16[512,256]{1,0:T(8,128)(2,1)S(1)} %bitcast.5), custom_call_target="tpu_custom_call" | custom-call | flops 268435456 | bytes 786504 | tf_op jit(solution)/shard_map/extend/extend/pallas_call | solution.py:332
  27.6 1.4 %collective-permute-start.6 = (bf16[4,64,256]{2,1,0:T(8,128)(2,1)S(1)}, bf16[4,64,256]{2,1,0:T(8,128)(2,1)S(1)}, u32[]{:S(2)}, u32[]{:S(2)}) collective-permute-start(bf16[4,64,256]{2,1,0:T(8,128)(2,1)S(1)} %get-tuple-element.66), channel_id=1, source_target_pairs={{0,4},{4,0},{8,12},{12,8},{16,20},{20,16},{24,28},{28,24},{1,5},{5... | collective-permute-start | bytes 393224 | tf_op jit(solution)/shard_map/extend/ppermute | solution.py:370
  29.0 7.2 %attend.2 = (bf16[256,512]{1,0:T(8,128)(2,1)S(1)}, bf16[256,512]{1,0:T(8,128)(2,1)S(1)}, bf16[256,512]{1,0:T(8,128)(2,1)S(1)}, bf16[256,512]{1,0:T(8,128)(2,1)S(...) custom-call(s32[18]{0:T(128)S(1)} %pad_add_fusion.plan_ref, bf16[2048,128]{1,0:T(8,128)(2,1)S(1)} %get-tuple-element.68.q_ref, ...), custom_call_target="tpu_custom_call" | custom-call | flops 1476395008 | bytes 5779528 | tf_op jit(solution)/shard_map/attend/attend/pallas_call | solution.py:332
  36.5 1.4 %collective-permute-done.7 = bf16[256,512]{1,0:T(8,128)(2,1)S(1)} collective-permute-done((bf16[256,512]{1,0:T(8,128)(2,1)S(1)}, bf16[256,512]{1,0:T(8,128)(2,1)S(1)}, u32[]{:S(2)}, u32[]{:S(2)}) %collective-permute-start.7) | collective-permute-done | bytes 262176 | tf_op jit(solution)/shard_map/reduce/ppermute | solution.py:370
  37.9 1.5 %collective-permute-start.9 = (bf16[256,512]{1,0:T(8,128)(2,1)S(1)}, bf16[256,512]{1,0:T(8,128)(2,1)S(1)}, u32[]{:S(2)}, u32[]{:S(2)}) collective-permute-start(bf16[256,512]{1,0:T(8,128)(2,1)S(1)} %add_convert_fusion.1), channel_id=1, source_target_pairs={{0,2},{1,3},{2,0},{3,1},{4,6},{5,7},{6,4},{7,5},{8,10},{9,11},{10,... | collective-permute-start | bytes 786440 | tf_op jit(solution)/shard_map/reduce/ppermute | solution.py:370
  39.5 7.1 %attend.3 = (bf16[256,512]{1,0:T(8,128)(2,1)S(1)}, bf16[256,512]{1,0:T(8,128)(2,1)S(1)}, bf16[256,512]{1,0:T(8,128)(2,1)S(1)}, bf16[256,512]{1,0:T(8,128)(2,1)S(1)}) custom-call(s32[18]{0:T(128)S(1)} %pad_add_fusion.plan_ref, bf16[2048,128]{1,0:T(8,128)(2,1)S(1)} %get-tuple-element.68.q_ref, bf16[512,256]{1,0:T(8,128)(2,1)S(1)} %get-tuple-element.57.kv_ref, ...), custom_call_target="tpu_custom_call" | custom-call | flops 1610612736 | bytes 5779528 | tf_op jit(solution)/shard_map/attend/attend/pallas_call | solution.py:332
  47.2 1.5 %collective-permute-done.10 = bf16[256,512]{1,0:T(8,128)(2,1)S(1)} collective-permute-done((bf16[256,512]{1,0:T(8,128)(2,1)S(1)}, bf16[256,512]{1,0:T(8,128)(2,1)S(1)}, u32[]{:S(2)}, u32[]{:S(2)}) %collective-permute-start.10) | collective-permute-done | bytes 262176 | tf_op jit(solution)/shard_map/reduce/ppermute | solution.py:370
  48.7 0.7 %collective-permute-start.11 = (bf16[256,512]{1,0:T(8,128)(2,1)S(1)}, bf16[256,512]{1,0:T(8,128)(2,1)S(1)}, u32[]{:S(2)}, u32[]{:S(2)}) collective-permute-start(bf16[256,512]{1,0:T(8,128)(2,1)S(1)} %add_convert_fusion), channel_id=1, source_target_pairs={{0,2},{1,3},{2,0},{3,1},{4,6},{5,7},{6,4},{7,5},{8,10},{9,11},{10,... | collective-permute-start | bytes 786440 | tf_op jit(solution)/shard_map/reduce/ppermute | solution.py:370
  49.4 4.8 %collective-permute-start.13 = (bf16[2,64,256]{2,1,0:T(8,128)(2,1)S(1)}, bf16[2,64,256]{2,1,0:T(8,128)(2,1)S(1)}, u32[]{:S(2)}, u32[]{:S(2)}) collective-permute-start(bf16[2,64,256]{2,1,0:T(8,128)(2,1)S(1)} %get-tuple-element.85), channel_id=1, source_target_pairs={{0,8},{4,12},{8,0},{12,4},{16,24},{20,28},{24,16},{28,20},{1,9},{5... | collective-permute-start | bytes 196616 | tf_op jit(solution)/shard_map/exchange/ppermute | solution.py:370
  54.2 2.4 %collective-permute-start.15 = (bf16[2,64,256]{2,1,0:T(8,128)(2,1)S(1)}, bf16[2,64,256]{2,1,0:T(8,128)(2,1)S(1)}, u32[]{:S(2)}, u32[]{:S(2)}) collective-permute-start(bf16[2,64,256]{2,1,0:T(8,128)(2,1)S(1)} %get-tuple-element.87), channel_id=1, source_target_pairs={{0,24},{4,28},{8,16},{12,20},{16,8},{20,12},{24,0},{28,4},{1,25},{... | collective-permute-start | bytes 196616 | tf_op jit(solution)/shard_map/exchange/ppermute | solution.py:370
  56.7 1.4 %finish.2.refs_0_ = bf16[512,512]{1,0:T(8,128)(2,1)} custom-call(s32[18]{0:T(128)S(1)} %pad_add_fusion.plan_ref, bf16[512,512]{1,0:T(8,128)(2,1)S(1)} %broadcast_maximum_fusion.x0.tokens_ref, bf16[256,512]{1,0:T(8,128)(2,1)S(1)} %get-tuple-element.79.near_ref, bf16[256,512]{1,0:T(8,128)(2,1)S(1)} %collective-permute-done.12.got_ref, ...), custom_call_target="tpu_custom_call" | custom-call | flops 524288 | bytes 1835080 | tf_op jit(solution)/shard_map/finish/finish/pallas_call | solution.py:332
  58.1 3.7 %collective-permute-done.14.refs_2_ = bf16[2,64,256]{2,1,0:T(8,128)(2,1)S(1)} collective-permute-done((bf16[2,64,256]{2,1,0:T(8,128)(2,1)S(1)}, bf16[2,64,256]{2,1,0:T(8,128)(2,1)S(1)}, u32[]{:S(2)}, u32[]{:S(2)}) %collective-permute-start.14) | collective-permute-done | bytes 65568 | tf_op jit(solution)/shard_map/exchange/ppermute | solution.py:370
  61.7 0.7 %place.1 = bf16[8,64,256]{2,1,0:T(8,128)(2,1)} custom-call(bf16[2,64,256]{2,1,0:T(8,128)(2,1)S(1)} %get-tuple-element.84.refs_0_, bf16[2,64,256]{2,1,0:T(8,128)(2,1)S(1)} %collective-permute-done.13.refs_1_, bf16[2,64,256]{2,1,0:T(8,128)(2,1)S(1)} %collective-permute-done.14.refs_2_, bf16[2,64,256]{2,1,0:T(8,128)(2,1)S(1)} %collective-permute-done.15.refs_3_), custom_call_target="tpu_custom_call" | custom-call | bytes 524288 | tf_op jit(solution)/shard_map/exchange/place/pallas_call | solution.py:332
  62.5 1.4 %finish.3 = bf16[512,512]{1,0:T(8,128)(2,1)} custom-call(s32[18]{0:T(128)S(1)} %pad_add_fusion.plan_ref, bf16[512,512]{1,0:T(8,128)(2,1)S(1)} %broadcast_maximum_fusion.x0.tokens_ref, bf16[256,512]{1,0:T(8,128)(2,1)S(1)} %get-tuple-element.71.near_ref, bf16[256,512]{1,0:T(8,128)(2,1)S(1)} %collective-permute-done.8.got_ref, ...), custom_call_target="tpu_custom_call", output_to_operand_aliasing={{}: (5, {})} | custom-call | flops 524288 | bytes 2359368 | tf_op jit(solution)/shard_map/finish/finish/pallas_call | solution.py:332
  (25 shorter events, 2.2 us)
Async XLA Ops:
  0.6 3.1 %collective-permute-start = (bf16[512,512]{1,0:T(8,128)(2,1)}, bf16[512,512]{1,0:T(8,128)(2,1)S(1)}, u32[]{:S(2)}, u32[]{:S(2)}) collective-permute-start(bf16[512,512]{1,0:T(8,128)(2,1)} %param.10), channel_id=1, source_target_pairs={{0,1},{1,0},{2,3},{3,2},{4,5},{5,4},{6,7},{7,6},{8,9},{9,8},{10,11... | collective-permute-start | bytes 1572872 | tf_op jit(solution)/shard_map/tokens_gather/ppermute | solution.py:370
  1.1 15.3 %collective-permute-start.1 = (bf16[512,512]{1,0:T(8,128)(2,1)}, bf16[512,512]{1,0:T(8,128)(2,1)S(1)}, u32[]{:S(2)}, u32[]{:S(2)}) collective-permute-start(bf16[512,512]{1,0:T(8,128)(2,1)} %param.10), channel_id=1, source_target_pairs={{0,2},{1,3},{2,0},{3,1},{4,6},{5,7},{6,4},{7,5},{8,10},{9,11},{10,... | collective-permute-start | bytes 1572872 | tf_op jit(solution)/shard_map/tokens_gather/ppermute | solution.py:370
  3.7 15.5 %all-to-all-start = ((bf16[8,64,256]{2,1,0:T(8,128)(2,1)}), bf16[8,64,256]{2,1,0:T(8,128)(2,1)S(1)}, u32[]{:S(2)}, u32[]{:S(2)}) async-start(bf16[8,64,256]{2,1,0:T(8,128)(2,1)} %param.19), calls=%async_computation | async-start | bytes 524288 | tf_op jit(solution)/shard_map/cache_gather/all_to_all | solution.py:373
  19.3 2.6 %collective-permute-start.2 = (bf16[512,512]{1,0:T(8,128)(2,1)S(1)}, bf16[512,512]{1,0:T(8,128)(2,1)S(1)}, u32[]{:S(2)}, u32[]{:S(2)}) collective-permute-start(bf16[512,512]{1,0:T(8,128)(2,1)S(1)} %collective-permute-done.1.x2), channel_id=1, source_target_pairs={{0,1},{1,0},{2,3},{3,2},{4,5},{5,4},{6,7},{7,6},{8,9},{9,8},{10,11... | collective-permute-start | bytes 1572872 | tf_op jit(solution)/shard_map/project/ppermute | solution.py:370
  20.1 7.4 %collective-permute-start.4 = (bf16[384,256]{1,0:T(8,128)(2,1)S(1)}, bf16[384,256]{1,0:T(8,128)(2,1)S(1)}, u32[]{:S(2)}, u32[]{:S(2)}) collective-permute-start(bf16[384,256]{1,0:T(8,128)(2,1)S(1)} %order.1.refs_1_), channel_id=1, source_target_pairs={{0,2},{1,3},{2,0},{3,1},{4,6},{5,7},{6,4},{7,5},{8,10},{9,11},{10,... | collective-permute-start | bytes 589832 | tf_op jit(solution)/shard_map/cache_gather/ppermute | solution.py:370
  21.7 7.3 %collective-permute-start.3 = (bf16[384,256]{1,0:T(8,128)(2,1)S(1)}, bf16[384,256]{1,0:T(8,128)(2,1)S(1)}, u32[]{:S(2)}, u32[]{:S(2)}) collective-permute-start(bf16[384,256]{1,0:T(8,128)(2,1)S(1)} %order.1.refs_1_), channel_id=1, source_target_pairs={{0,1},{1,0},{2,3},{3,2},{4,5},{5,4},{6,7},{7,6},{8,9},{9,8},{10,11... | collective-permute-start | bytes 589832 | tf_op jit(solution)/shard_map/cache_gather/ppermute | solution.py:370
  27.5 1.5 %collective-permute-start.5 = (bf16[384,256]{1,0:T(8,128)(2,1)S(1)}, bf16[384,256]{1,0:T(8,128)(2,1)S(1)}, u32[]{:S(2)}, u32[]{:S(2)}) collective-permute-start(bf16[384,256]{1,0:T(8,128)(2,1)S(1)} %collective-permute-done.4.refs_3_), channel_id=1, source_target_pairs={{0,1},{1,0},{2,3},{3,2},{4,5},{5,4},{6,7},{7,6},{8,9},{9,8},{10,11... | collective-permute-start | bytes 589832 | tf_op jit(solution)/shard_map/extend/ppermute | solution.py:370
  27.6 8.7 %collective-permute-start.6 = (bf16[4,64,256]{2,1,0:T(8,128)(2,1)S(1)}, bf16[4,64,256]{2,1,0:T(8,128)(2,1)S(1)}, u32[]{:S(2)}, u32[]{:S(2)}) collective-permute-start(bf16[4,64,256]{2,1,0:T(8,128)(2,1)S(1)} %get-tuple-element.66), channel_id=1, source_target_pairs={{0,4},{4,0},{8,12},{12,8},{16,20},{20,16},{24,28},{28,24},{1,5},{5... | collective-permute-start | bytes 393224 | tf_op jit(solution)/shard_map/extend/ppermute | solution.py:370
  36.3 1.6 %collective-permute-start.7 = (bf16[256,512]{1,0:T(8,128)(2,1)S(1)}, bf16[256,512]{1,0:T(8,128)(2,1)S(1)}, u32[]{:S(2)}, u32[]{:S(2)}) collective-permute-start(bf16[256,512]{1,0:T(8,128)(2,1)S(1)} %get-tuple-element.67), channel_id=1, source_target_pairs={{0,1},{1,0},{2,3},{3,2},{4,5},{5,4},{6,7},{7,6},{8,9},{9,8},{10,11... | collective-permute-start | bytes 786440 | tf_op jit(solution)/shard_map/reduce/ppermute | solution.py:370
  37.9 9.3 %collective-permute-start.9 = (bf16[256,512]{1,0:T(8,128)(2,1)S(1)}, bf16[256,512]{1,0:T(8,128)(2,1)S(1)}, u32[]{:S(2)}, u32[]{:S(2)}) collective-permute-start(bf16[256,512]{1,0:T(8,128)(2,1)S(1)} %add_convert_fusion.1), channel_id=1, source_target_pairs={{0,2},{1,3},{2,0},{3,1},{4,6},{5,7},{6,4},{7,5},{8,10},{9,11},{10,... | collective-permute-start | bytes 786440 | tf_op jit(solution)/shard_map/reduce/ppermute | solution.py:370
  39.5 14.8 %collective-permute-start.12 = (bf16[256,512]{1,0:T(8,128)(2,1)S(1)}, bf16[256,512]{1,0:T(8,128)(2,1)S(1)}, u32[]{:S(2)}, u32[]{:S(2)}) collective-permute-start(bf16[256,512]{1,0:T(8,128)(2,1)S(1)} %get-tuple-element.80), channel_id=1, source_target_pairs={{0,1},{1,0},{2,3},{3,2},{4,5},{5,4},{6,7},{7,6},{8,9},{9,8},{10,11... | collective-permute-start | bytes 786440 | tf_op jit(solution)/shard_map/reduce/ppermute | solution.py:370
  46.6 15.9 %collective-permute-start.8 = (bf16[256,512]{1,0:T(8,128)(2,1)S(1)}, bf16[256,512]{1,0:T(8,128)(2,1)S(1)}, u32[]{:S(2)}, u32[]{:S(2)}) collective-permute-start(bf16[256,512]{1,0:T(8,128)(2,1)S(1)} %get-tuple-element.72), channel_id=1, source_target_pairs={{0,1},{1,0},{2,3},{3,2},{4,5},{5,4},{6,7},{7,6},{8,9},{9,8},{10,11... | collective-permute-start | bytes 786440 | tf_op jit(solution)/shard_map/reduce/ppermute | solution.py:370
  47.1 1.5 %collective-permute-start.10 = (bf16[256,512]{1,0:T(8,128)(2,1)S(1)}, bf16[256,512]{1,0:T(8,128)(2,1)S(1)}, u32[]{:S(2)}, u32[]{:S(2)}) collective-permute-start(bf16[256,512]{1,0:T(8,128)(2,1)S(1)} %get-tuple-element.75), channel_id=1, source_target_pairs={{0,1},{1,0},{2,3},{3,2},{4,5},{5,4},{6,7},{7,6},{8,9},{9,8},{10,11... | collective-permute-start | bytes 786440 | tf_op jit(solution)/shard_map/reduce/ppermute | solution.py:370
  48.7 13.7 %collective-permute-start.11 = (bf16[256,512]{1,0:T(8,128)(2,1)S(1)}, bf16[256,512]{1,0:T(8,128)(2,1)S(1)}, u32[]{:S(2)}, u32[]{:S(2)}) collective-permute-start(bf16[256,512]{1,0:T(8,128)(2,1)S(1)} %add_convert_fusion), channel_id=1, source_target_pairs={{0,2},{1,3},{2,0},{3,1},{4,6},{5,7},{6,4},{7,5},{8,10},{9,11},{10,... | collective-permute-start | bytes 786440 | tf_op jit(solution)/shard_map/reduce/ppermute | solution.py:370
  49.4 8.6 %collective-permute-start.13 = (bf16[2,64,256]{2,1,0:T(8,128)(2,1)S(1)}, bf16[2,64,256]{2,1,0:T(8,128)(2,1)S(1)}, u32[]{:S(2)}, u32[]{:S(2)}) collective-permute-start(bf16[2,64,256]{2,1,0:T(8,128)(2,1)S(1)} %get-tuple-element.85), channel_id=1, source_target_pairs={{0,8},{4,12},{8,0},{12,4},{16,24},{20,28},{24,16},{28,20},{1,9},{5... | collective-permute-start | bytes 196616 | tf_op jit(solution)/shard_map/exchange/ppermute | solution.py:370
  54.2 7.5 %collective-permute-start.14 = (bf16[2,64,256]{2,1,0:T(8,128)(2,1)S(1)}, bf16[2,64,256]{2,1,0:T(8,128)(2,1)S(1)}, u32[]{:S(2)}, u32[]{:S(2)}) collective-permute-start(bf16[2,64,256]{2,1,0:T(8,128)(2,1)S(1)} %get-tuple-element.86), channel_id=1, source_target_pairs={{0,16},{4,20},{8,24},{12,28},{16,0},{20,4},{24,8},{28,12},{1,17},{... | collective-permute-start | bytes 196616 | tf_op jit(solution)/shard_map/exchange/ppermute | solution.py:370
  54.2 7.5 %collective-permute-start.15 = (bf16[2,64,256]{2,1,0:T(8,128)(2,1)S(1)}, bf16[2,64,256]{2,1,0:T(8,128)(2,1)S(1)}, u32[]{:S(2)}, u32[]{:S(2)}) collective-permute-start(bf16[2,64,256]{2,1,0:T(8,128)(2,1)S(1)} %get-tuple-element.87), channel_id=1, source_target_pairs={{0,24},{4,28},{8,16},{12,20},{16,8},{20,12},{24,0},{28,4},{1,25},{... | collective-permute-start | bytes 196616 | tf_op jit(solution)/shard_map/exchange/ppermute | solution.py:370
